TPU v7x, 32 devices: a whole 2x2x4 slice. The times are simulated.
32 devices in a mesh: gx: 4 (over y, x), gy: 8 (over z, core).
Axes of the slice: x: 2, y: 2, z: 4, core: 2. Of those that a mesh axis runs over, the one named last changes fastest.
Arguments:
- coords: float32 [3, 131072], P(None, ('gx', 'gy')), may hold values from 0 to 8
- noise: float32 [131072], P(('gx', 'gy')), may hold values from 0.5 to 2
- order: int32 [4, 32768], P('gx', 'gy'), may hold values from 0 to 32767, as said below
- probes: bfloat16 [64, 131072], P(None, ('gx', 'gy')), may hold values from -5 to 5
- factors: bfloat16 [7, 2, 32, 131072], P(None, None, None, ('gx', 'gy')), may hold values from -1 to 1
Outputs:
- product: float32 [64, 131072], P(None, ('gx', 'gy'))
Inputs may be any that keep to these rules, and one draw needn't show every extreme that they name: Each row of order lists every number from 0 to 32767 once; every run of 4096 tree positions starting at a multiple of 4096 takes exactly 512 numbers from each run of 4096 input indices starting at a multiple of 4096.
All inputs are finite; a program needn't handle non-finite values.
Results may differ from a plain program's by a relative error of at most 0.0029.
Values may be sent and summed in bfloat16 or wider, within the bound.
No kernel may reach another device: no remote copies, remote signals or barrier semaphores. Data moves between devices by JAX's collectives and lax.ppermute only.
A program may use at most 128 MiB of HBM per device.

v0:
```python
import jax
import jax.numpy as jnp
from jax import lax
from jax.sharding import PartitionSpec as P

LEAF = 1024


SQRT_THREE = 1.7320508075688772


def swapped(array, axis, stride):
    return lax.ppermute(array, axis, [(i, i ^ 1 << stride) for i in range(lax.axis_size(axis))])


def leaf_kernel(spots, spread):
    square = (spots[0][:, None] - spots[0][None, :]) ** 2
    square = square + (spots[1][:, None] - spots[1][None, :]) ** 2
    square = square + (spots[2][:, None] - spots[2][None, :]) ** 2
    scaled = jnp.sqrt(square) * SQRT_THREE
    return ((1.0 + scaled) * jnp.exp(-scaled) + jnp.diag(spread)).astype(jnp.bfloat16)


def local_term(pair, probes, width):
    total = probes.shape[1]
    nodes = total // width
    rank_size = pair.shape[1]
    count = probes.shape[0]
    right = pair[1].reshape(rank_size, nodes, width)
    left = pair[0].reshape(rank_size, nodes, width)
    vectors = probes.reshape(count, nodes, width)
    coeff = jnp.einsum("rkn,pkn->krp", right, vectors, preferred_element_type=jnp.float32)
    sibling = (
        coeff.reshape(nodes // 2, 2, rank_size, count)[:, ::-1]
        .reshape(nodes, rank_size, count)
        .astype(jnp.bfloat16)
    )
    return jnp.einsum("rkn,krp->pkn", left, sibling, preferred_element_type=jnp.float32).reshape(
        count, total
    )


def pair_inner(values, step_bit):
    return swapped(values, "gy", step_bit)


def sibling_inner(values, step_bit):
    return swapped(values.astype(jnp.bfloat16), "gy", step_bit)


def local(coords, noise, order, probes, factors):
    points = probes.shape[1]
    picks = order[0]
    whole_coords, whole_noise = (
        lax.all_gather(coords, "gy", axis=1, tiled=True),
        lax.all_gather(noise, "gy", axis=0, tiled=True),
    )
    tree_coords = jnp.take(whole_coords, picks, axis=1)
    tree_noise = jnp.take(whole_noise, picks, axis=0)
    blocks = []
    for leaf_index in range(points // LEAF):
        start = leaf_index * LEAF
        kernel = leaf_kernel(tree_coords[:, start : start + LEAF], tree_noise[start : start + LEAF])
        blocks.append(
            jnp.dot(probes[:, start : start + LEAF], kernel, preferred_element_type=jnp.float32)
        )
    product = jnp.concatenate(blocks, axis=1)
    local_levels = (points // LEAF).bit_length() - 1
    for tier_index in range(local_levels):
        product = product + local_term(factors[tier_index], probes, LEAF * 2**tier_index)
    inner_bits = lax.axis_size("gy").bit_length() - 1
    outer_bits = lax.axis_size("gx").bit_length() - 1
    device_levels = inner_bits + outer_bits
    level_terms = [
        jnp.einsum(
            "rn,pn->rp",
            factors[local_levels + height, 1],
            probes,
            preferred_element_type=jnp.float32,
        )
        for height in range(device_levels)
    ]
    siblings = [None] * device_levels
    upper_terms = []
    for height in range(device_levels):
        running = level_terms[height]
        for step_bit in range(min(height, inner_bits)):
            running = running + pair_inner(running, step_bit)
        if height < inner_bits:
            siblings[height] = sibling_inner(running, height)
        else:
            upper_terms.append(running)
    pending = jnp.stack(upper_terms)
    for step_bit in range(outer_bits):
        siblings[inner_bits + step_bit] = swapped(
            pending[step_bit].astype(jnp.bfloat16), "gx", step_bit
        )
        if step_bit + 1 < outer_bits:
            arrived = swapped(pending[step_bit + 1 :], "gx", step_bit)
            pending = jnp.concatenate(
                [pending[: step_bit + 1], pending[step_bit + 1 :] + arrived], axis=0
            )
    for height in range(device_levels):
        product = product + jnp.einsum(
            "rn,rp->pn",
            factors[local_levels + height, 0],
            siblings[height],
            preferred_element_type=jnp.float32,
        )
    return product


def solution(mesh):
    return jax.shard_map(
        local,
        mesh=mesh,
        in_specs=(
            P(None, ("gx", "gy")),
            P(("gx", "gy")),
            P("gx", "gy"),
            P(None, ("gx", "gy")),
            P(None, None, None, ("gx", "gy")),
        ),
        out_specs=P(None, ("gx", "gy")),
        check_vma=False,
    )
```

profile of v0, /device:TPU:0, one launch (start us, length us, event | category | flops | bytes accessed | tf_op | source)
XLA Modules:
  0.0 253.8 jit_solution(7694279115920790891)
XLA Ops:
  0.0 1.4 fusion.21
  1.4 0.5 collective-permute-start.10
  1.9 1.4 fusion.25
  3.4 1.4 fusion.29
  4.7 0.5 collective-permute-start.3
  5.2 1.4 fusion.33
  6.7 1.4 convolution_convert_fusion
  8.1 0.5 collective-permute-start
  8.6 1.3 fusion.68
  9.9 15.3 %all_gather.7 = f32[32768]{0:T(1024)S(1)} all-gather(f32[4096]{0:T(1024)S(1)} %copy-done.3), channel_id=1, replica_groups=mesh['gx'=4,'gy'=8] {'gy'}, dimensions={0}, use_global_device_ids=true | all-gather | bytes 147456 | tf_op jit(solution)/shard_map/all_gather | solution.py:56
  25.1 0.6 copy.25
  25.8 140.4 %all_gather.6 = f32[3,32768]{0,1:T(8,128)} all-gather(f32[3,4096]{0,1:T(8,128)S(1)} %copy.25), channel_id=1, replica_groups=mesh['gx'=4,'gy'=8] {'gy'}, dimensions={1}, use_global_device_ids=true | all-gather | bytes 442368 | tf_op jit(solution)/shard_map/all_gather | solution.py:55
  166.2 23.0 %gather_fusion.1 = f32[4096]{0:T(1024)S(1)} fusion(f32[32768]{0:T(1024)S(1)} %all_gather.7, s32[4096]{0:T(1024)S(1)} %broadcast_clamp_fusion), kind=kCustom, calls=%fused_computation.1 | custom fusion | bytes 49152 | tf_op jit(solution)/shard_map/jit(_take)/gather | solution.py:59
  189.2 16.5 %gather_fusion = f32[4096,3]{1,0:T(8,128)S(1)} fusion(f32[3,32768]{0,1:T(8,128)} %all_gather.6, s32[4096]{0:T(1024)S(1)} %broadcast_clamp_fusion), kind=kCustom, calls=%fused_computation | custom fusion | bytes 114688 | tf_op jit(solution)/shard_map/jit(_take)/gather | solution.py:58
  205.8 2.3 select_bitcast_fusion
  208.1 2.8 %slice_reduce_fusion.11 = (f32[1024]{0:T(1024)S(1)}, f32[1024]{0:T(1024)S(1)}, f32[1024]{0:T(1024)S(1)}, f32[1024]{0:T(1024)S(1)}, f32[1024]{0:T(1024)S(1)}, /*i...) fusion(f32[3,4096]{0,1:T(8,128)S(1)} %select_bitcast_fusion), kind=kLoop, calls=%fused_computation.43 | loop fusion | bytes 98304 | tf_op jit(solution)/shard_map/slice | solution.py:17
  210.9 0.2 reshape_squeeze.12
  211.1 0.3 fusion.16
  211.4 0.2 reshape_squeeze.13
  211.6 0.2 reshape_squeeze.14
  211.8 0.3 fusion.13
  212.1 0.2 reshape_squeeze.15
  212.2 0.3 convolution_bitcast_fusion.1
  212.6 3.3 %fusion.11 = f32[64,1024]{1,0:T(8,128)S(1)} fusion(f32[1024]{0:T(1024)S(1)} %get-tuple-element.23, f32[1024]{0:T(1024)S(1)} %get-tuple-element.15, f32[1024]{0:T(1024)S(1)} %get-tuple-element.16, f32[1024]{0:T(1024)S(1)} %get-tuple-element.5, bf16[64,4096]{1,0:T(8,128)(2,1)S(1)} %copy-done), kind=kOutput, calls=%fused_computation.22 | convolution fusion | flops 150994944 | bytes 421888 | tf_op jit(solution)/shard_map/dot_general | solution.py:65
  215.9 3.3 %fusion.10 = f32[64,1024]{1,0:T(8,128)S(1)} fusion(f32[1024]{0:T(1024)S(1)} %get-tuple-element.26, f32[1024]{0:T(1024)S(1)} %get-tuple-element.12, f32[1024]{0:T(1024)S(1)} %get-tuple-element.13, f32[1024]{0:T(1024)S(1)} %get-tuple-element.14, bf16[64,4096]{1,0:T(8,128)(2,1)S(1)} %copy-done), kind=kOutput, calls=%fused_computation.21 | convolution fusion | flops 150994944 | bytes 421888 | tf_op jit(solution)/shard_map/dot_general | solution.py:65
  219.1 3.5 %fusion.9 = f32[64,1024]{1,0:T(8,128)S(1)} fusion(f32[1024]{0:T(1024)S(1)} %get-tuple-element.25, f32[1024]{0:T(1024)S(1)} %get-tuple-element.9, f32[1024]{0:T(1024)S(1)} %get-tuple-element.10, f32[1024]{0:T(1024)S(1)} %get-tuple-element.11, bf16[64,4096]{1,0:T(8,128)(2,1)S(1)} %copy-done), kind=kOutput, calls=%fused_computation.20 | convolution fusion | flops 150994944 | bytes 421888 | tf_op jit(solution)/shard_map/dot_general | solution.py:65
  222.6 3.3 %fusion.8 = f32[64,1024]{1,0:T(8,128)S(1)} fusion(f32[1024]{0:T(1024)S(1)} %get-tuple-element.24, f32[1024]{0:T(1024)S(1)} %get-tuple-element.6, f32[1024]{0:T(1024)S(1)} %get-tuple-element.7, f32[1024]{0:T(1024)S(1)} %get-tuple-element.8, bf16[64,4096]{1,0:T(8,128)(2,1)S(1)} %copy-done), kind=kOutput, calls=%fused_computation.19 | convolution fusion | flops 150994944 | bytes 421888 | tf_op jit(solution)/shard_map/dot_general | solution.py:65
  225.9 0.4 convolution_bitcast_fusion
  226.4 2.4 collective-permute-start.11
  229.0 2.1 collective-permute-start.4
  231.1 0.1 collective-permute-start.2
  231.2 1.7 collective-permute-done.4
  232.9 3.8 %collective-permute-start.5 = (bf16[32,64]{1,0:T(8,128)(2,1)S(1)}, bf16[32,64]{1,0:T(8,128)(2,1)S(1)}, u32[]{:S(2)}, u32[]{:S(2)}) collective-permute-start(bf16[32,64]{1,0:T(8,128)(2,1)S(1)} %add_convert_fusion.18), channel_id=1, source_target_pairs={{0,4},{1,5},{2,6},{3,7},{4,0},{5,1},{6,2},{7,3},{8,12},{9,13},{10,... | collective-permute-start | bytes 12296 | tf_op jit(solution)/shard_map/ppermute | solution.py:13
  236.7 1.3 fusion.31
  238.0 2.0 collective-permute-start.12
  240.0 1.1 collective-permute-start.8
  241.0 1.3 fusion.27
  242.3 0.4 collective-permute-done.12
  242.7 1.5 collective-permute-start.13
  244.2 0.5 collective-permute-done.8
  244.7 1.5 collective-permute-start.9
  246.2 0.3 collective-permute-done.13
  246.4 1.5 collective-permute-start.14
  248.0 0.4 collective-permute-done.9
  248.3 1.3 fusion.23
  249.6 0.5 collective-permute-done.14
  250.1 1.3 fusion.19
  251.4 2.4 fusion.3
  (38 shorter events, 0.5 us)
Async XLA Ops:
  0.0 9.8 %copy-start.2 = (s32[1,4096]{1,0:T(1,128)S(1)}, s32[1,4096]{1,0:T(1,128)}, u32[]{:S(2)}) copy-start(s32[1,4096]{1,0:T(1,128)} %param.7) | copy-start | bytes 49156
  0.0 9.9 %copy-start.3 = (f32[4096]{0:T(1024)S(1)}, f32[4096]{0:T(1024)}, u32[]{:S(2)}) copy-start(f32[4096]{0:T(1024)} %param.6) | copy-start | bytes 49156
  0.0 25.1 %copy-start.1 = (f32[3,4096]{1,0:T(4,128)S(1)}, f32[3,4096]{1,0:T(4,128)}, u32[]{:S(2)}) copy-start(f32[3,4096]{1,0:T(4,128)} %param.5) | copy-start | bytes 147460
  1.4 225.0 %collective-permute-start.10 = (f32[32,64]{1,0:T(8,128)S(1)}, f32[32,64]{1,0:T(8,128)S(1)}, u32[]{:S(2)}, u32[]{:S(2)}) collective-permute-start(f32[32,64]{1,0:T(8,128)S(1)} %fusion.21), channel_id=1, source_target_pairs={{0,1},{1,0},{2,3},{3,2},{4,5},{5,4},{6,7},{7,6},{8,9},{9,8},{10,11... | collective-permute-start | bytes 24584 | tf_op jit(solution)/shard_map/ppermute | solution.py:13
  3.3 225.6 %collective-permute-start.6 = (f32[32,64]{1,0:T(8,128)S(1)}, f32[32,64]{1,0:T(8,128)S(1)}, u32[]{:S(2)}, u32[]{:S(2)}) collective-permute-start(f32[32,64]{1,0:T(8,128)S(1)} %fusion.25), channel_id=1, source_target_pairs={{0,1},{1,0},{2,3},{3,2},{4,5},{5,4},{6,7},{7,6},{8,9},{9,8},{10,11... | collective-permute-start | bytes 24584 | tf_op jit(solution)/shard_map/ppermute | solution.py:13
  4.7 224.2 %collective-permute-start.3 = (f32[32,64]{1,0:T(8,128)S(1)}, f32[32,64]{1,0:T(8,128)S(1)}, u32[]{:S(2)}, u32[]{:S(2)}) collective-permute-start(f32[32,64]{1,0:T(8,128)S(1)} %fusion.29), channel_id=1, source_target_pairs={{0,1},{1,0},{2,3},{3,2},{4,5},{5,4},{6,7},{7,6},{8,9},{9,8},{10,11... | collective-permute-start | bytes 24584 | tf_op jit(solution)/shard_map/ppermute | solution.py:13
  6.6 224.4 %collective-permute-start.1 = (f32[32,64]{1,0:T(8,128)S(1)}, f32[32,64]{1,0:T(8,128)S(1)}, u32[]{:S(2)}, u32[]{:S(2)}) collective-permute-start(f32[32,64]{1,0:T(8,128)S(1)} %fusion.33), channel_id=1, source_target_pairs={{0,1},{1,0},{2,3},{3,2},{4,5},{5,4},{6,7},{7,6},{8,9},{9,8},{10,11... | collective-permute-start | bytes 24584 | tf_op jit(solution)/shard_map/ppermute | solution.py:13
  8.1 243.3 %collective-permute-start = (bf16[32,64]{1,0:T(8,128)(2,1)S(1)}, bf16[32,64]{1,0:T(8,128)(2,1)S(1)}, u32[]{:S(2)}, u32[]{:S(2)}) collective-permute-start(bf16[32,64]{1,0:T(8,128)(2,1)S(1)} %convolution_convert_fusion), channel_id=1, source_target_pairs={{0,1},{1,0},{2,3},{3,2},{4,5},{5,4},{6,7},{7,6},{8,9},{9,8},{10,11... | collective-permute-start | bytes 12296 | tf_op jit(solution)/shard_map/ppermute | solution.py:13
  208.1 3.0 %copy-start = (bf16[64,4096]{1,0:T(8,128)(2,1)S(1)}, bf16[64,4096]{1,0:T(8,128)(2,1)}, u32[]{:S(2)}) copy-start(bf16[64,4096]{1,0:T(8,128)(2,1)} %param.8) | copy-start | bytes 1572868
  226.4 11.5 %collective-permute-start.11 = (f32[32,64]{1,0:T(8,128)S(1)}, f32[32,64]{1,0:T(8,128)S(1)}, u32[]{:S(2)}, u32[]{:S(2)}) collective-permute-start(f32[32,64]{1,0:T(8,128)S(1)} %add.156), channel_id=1, source_target_pairs={{0,2},{1,3},{2,0},{3,1},{4,6},{5,7},{6,4},{7,5},{8,10},{9,11},{10,... | collective-permute-start | bytes 24584 | tf_op jit(solution)/shard_map/ppermute | solution.py:13
  228.9 11.1 %collective-permute-start.7 = (f32[32,64]{1,0:T(8,128)S(1)}, f32[32,64]{1,0:T(8,128)S(1)}, u32[]{:S(2)}, u32[]{:S(2)}) collective-permute-start(f32[32,64]{1,0:T(8,128)S(1)} %add.152), channel_id=1, source_target_pairs={{0,2},{1,3},{2,0},{3,1},{4,6},{5,7},{6,4},{7,5},{8,10},{9,11},{10,... | collective-permute-start | bytes 24584 | tf_op jit(solution)/shard_map/ppermute | solution.py:13
  229.0 3.9 %collective-permute-start.4 = (f32[32,64]{1,0:T(8,128)S(1)}, f32[32,64]{1,0:T(8,128)S(1)}, u32[]{:S(2)}, u32[]{:S(2)}) collective-permute-start(f32[32,64]{1,0:T(8,128)S(1)} %add.149), channel_id=1, source_target_pairs={{0,2},{1,3},{2,0},{3,1},{4,6},{5,7},{6,4},{7,5},{8,10},{9,11},{10,... | collective-permute-start | bytes 24584 | tf_op jit(solution)/shard_map/ppermute | solution.py:13
  231.1 5.6 %collective-permute-start.2 = (bf16[32,64]{1,0:T(8,128)(2,1)S(1)}, bf16[32,64]{1,0:T(8,128)(2,1)S(1)}, u32[]{:S(2)}, u32[]{:S(2)}) collective-permute-start(bf16[32,64]{1,0:T(8,128)(2,1)S(1)} %add_convert_fusion.19), channel_id=1, source_target_pairs={{0,2},{1,3},{2,0},{3,1},{4,6},{5,7},{6,4},{7,5},{8,10},{9,11},{10,... | collective-permute-start | bytes 12296 | tf_op jit(solution)/shard_map/ppermute | solution.py:13
  232.9 8.2 %collective-permute-start.5 = (bf16[32,64]{1,0:T(8,128)(2,1)S(1)}, bf16[32,64]{1,0:T(8,128)(2,1)S(1)}, u32[]{:S(2)}, u32[]{:S(2)}) collective-permute-start(bf16[32,64]{1,0:T(8,128)(2,1)S(1)} %add_convert_fusion.18), channel_id=1, source_target_pairs={{0,4},{1,5},{2,6},{3,7},{4,0},{5,1},{6,2},{7,3},{8,12},{9,13},{10,... | collective-permute-start | bytes 12296 | tf_op jit(solution)/shard_map/ppermute | solution.py:13
  238.0 4.7 %collective-permute-start.12 = (f32[32,64]{1,0:T(8,128)S(1)}, f32[32,64]{1,0:T(8,128)S(1)}, u32[]{:S(2)}, u32[]{:S(2)}) collective-permute-start(f32[32,64]{1,0:T(8,128)S(1)} %add.157), channel_id=1, source_target_pairs={{0,4},{1,5},{2,6},{3,7},{4,0},{5,1},{6,2},{7,3},{8,12},{9,13},{10,... | collective-permute-start | bytes 24584 | tf_op jit(solution)/shard_map/ppermute | solution.py:13
  240.0 4.7 %collective-permute-start.8 = (f32[32,64]{1,0:T(8,128)S(1)}, f32[32,64]{1,0:T(8,128)S(1)}, u32[]{:S(2)}, u32[]{:S(2)}) collective-permute-start(f32[32,64]{1,0:T(8,128)S(1)} %add.153), channel_id=1, source_target_pairs={{0,4},{1,5},{2,6},{3,7},{4,0},{5,1},{6,2},{7,3},{8,12},{9,13},{10,... | collective-permute-start | bytes 24584 | tf_op jit(solution)/shard_map/ppermute | solution.py:13
  242.7 3.7 %collective-permute-start.13 = (f32[1,32,64]{2,1,0:T(8,128)S(1)}, f32[1,32,64]{2,1,0:T(8,128)S(1)}, u32[]{:S(2)}, u32[]{:S(2)}) collective-permute-start(f32[1,32,64]{2,1,0:T(8,128)S(1)} %add_bitcast_fusion), channel_id=1, source_target_pairs={{0,8},{8,0},{16,24},{24,16},{1,9},{9,1},{17,25},{25,17},{2,10},{10... | collective-permute-start | bytes 24584 | tf_op jit(solution)/shard_map/ppermute | solution.py:13
  244.7 3.7 %collective-permute-start.9 = (bf16[32,64]{1,0:T(8,128)(2,1)S(1)}, bf16[32,64]{1,0:T(8,128)(2,1)S(1)}, u32[]{:S(2)}, u32[]{:S(2)}) collective-permute-start(bf16[32,64]{1,0:T(8,128)(2,1)S(1)} %add_convert_fusion.17), channel_id=1, source_target_pairs={{0,8},{8,0},{16,24},{24,16},{1,9},{9,1},{17,25},{25,17},{2,10},{10... | collective-permute-start | bytes 12296 | tf_op jit(solution)/shard_map/ppermute | solution.py:13
  246.4 3.7 %collective-permute-start.14 = (bf16[32,64]{1,0:T(8,128)(2,1)S(1)}, bf16[32,64]{1,0:T(8,128)(2,1)S(1)}, u32[]{:S(2)}, u32[]{:S(2)}) collective-permute-start(bf16[32,64]{1,0:T(8,128)(2,1)S(1)} %fusion.55), channel_id=1, source_target_pairs={{0,16},{8,24},{16,0},{24,8},{1,17},{9,25},{17,1},{25,9},{2,18},{10... | collective-permute-start | bytes 12296 | tf_op jit(solution)/shard_map/ppermute | solution.py:13
where the time goes:
time: 254 us
  blocking collectives  156 us (61%)
  local copies, waits for them, and re-layouts  45.2 us (18%)
  matrix products  28.9 us (11%)
  starting transfers between devices  17.7 us (7%)
  waiting for transfers between devices  3.7 us (1%)
    all_gather x1, blocking collectives, local(): lax.all_gather(coords, 'gy', axis=1, tiled=True)  140 us
    gather x1, local copies, waits for them, and re-layouts, local(): tree_noise = jnp.take(whole_noise, picks, axis=0)  23 us
    ppermute x15, starting transfers between devices, swapped(): lax.ppermute(array, axis, [(i, i ^ 1 << stride) for i in range(lax.axis_s...  17.7 us
    gather x1, local copies, waits for them, and re-layouts, local(): tree_coords = jnp.take(whole_coords, picks, axis=1)  16.5 us
    all_gather x1, blocking collectives, local(): lax.all_gather(noise, 'gy', axis=0, tiled=True)  15.3 us
    dot_general x4, matrix products, local(): jnp.dot(probes[:, start:start + LEAF], kernel, preferred_element_type=jnp...  13.3 us
    dot_general x5, matrix products, local(): jnp.einsum('rn,rp->pn', factors[local_levels + height, 0], siblings[heigh...  7.48 us
    dot_general x5, matrix products, local(): jnp.einsum('rn,pn->rp', factors[local_levels + height, 1], probes, prefer...  6.92 us
  transfers between devices with their start and end apart: 15, of which 6 were waited for; matrix products, arithmetic and copies ran while one was open for 29% of the time, Pallas kernels for 0%

commit v1 on v0

v1 whole, which is shorter than its diff:
```python
import functools

import jax
import jax.numpy as jnp
from jax import lax
from jax.experimental import pallas as pl
from jax.experimental.pallas import tpu as pltpu
from jax.sharding import PartitionSpec as P

LEAF = 1024
TILE = 256
LANES = 256
STRIP = 128
NOISE_SCALE = 65535.0 / 2.0
OFFSET = 32768.0
SQRT_THREE = 1.7320508075688772
LOG2_E = 1.4426950408889634
LN_2 = 0.6931471805599453
LOG2_LN_2 = -0.5287663729448977
FEATURE_STEP = 2.0**-11
COORD_SCALE = SQRT_THREE * LOG2_E / FEATURE_STEP
COORD_MIDDLE = 80.0
COEFF_STEPS = 32760.0
MIB = 1024 * 1024


def exchanged(array, axis, mask):
    return lax.ppermute(array, axis, [(i, i ^ mask) for i in range(lax.axis_size(axis))])


def rounded_up(value, multiple):
    return -(-value // multiple) * multiple


def message_width(rank, outer_bits):
    return rounded_up(rank * (2 + outer_bits), 128)


def message_kernel(local_levels, inner_bits, factors_ref, probes_ref, coords_ref, noise_ref, *rest):
    message_refs, (right, vectors, spots, spread, right_sems, vector_sems, point_sems) = (
        rest[:-7],
        rest[-7:],
    )
    _, _, rank, points = factors_ref.shape
    count = probes_ref.shape[0]
    leaves = points // LEAF
    heights = right.shape[1]
    outer_bits = heights - inner_bits
    point_copies = [
        pltpu.make_async_copy(coords_ref, spots, point_sems.at[0]),
        pltpu.make_async_copy(noise_ref, spread, point_sems.at[1]),
    ]
    copies = []
    for leaf in range(leaves):
        span = pl.ds(leaf * LEAF, LEAF)
        copies.append(
            (
                pltpu.make_async_copy(
                    factors_ref.at[pl.ds(local_levels, heights), 1, :, span],
                    right.at[leaf],
                    right_sems.at[leaf],
                ),
                pltpu.make_async_copy(
                    probes_ref.at[:, span], vectors.at[leaf], vector_sems.at[leaf]
                ),
            )
        )
    for copy in point_copies:
        copy.start()
    for pair in copies:
        pair[0].start()
        pair[1].start()
    for copy in point_copies:
        copy.wait()

    sub = points // LANES
    lines = []
    for which in range(4):
        source = spots if which < 3 else spread
        scale = COORD_SCALE if which < 3 else NOISE_SCALE
        line = which if which < 3 else 0
        for at in range(sub):
            lines.append(source[line : line + 1, at * LANES : (at + 1) * LANES] * scale)
    coded = (jnp.round(jnp.concatenate(lines, axis=0)) - OFFSET).astype(jnp.int32).astype(jnp.int16)
    for message_ref in message_refs:
        message_ref[: 4 * sub] = coded

    upper = None
    for leaf in range(leaves):
        copies[leaf][0].wait()
        copies[leaf][1].wait()
        part = lax.dot_general(
            right[leaf].reshape(heights * rank, LEAF),
            vectors[leaf],
            (((1,), (1,)), ((), ())),
            preferred_element_type=jnp.float32,
        )
        upper = part if upper is None else upper + part
    upper = upper.T

    largest = jnp.max(jnp.abs(upper), axis=0, keepdims=True)
    power = jnp.ceil(jnp.log(jnp.maximum(largest, 2.0**-60)) * LOG2_E)
    fixed = jnp.round(upper * (COEFF_STEPS * jnp.exp2(-power)))
    wide = message_width(rank, outer_bits)
    pieces_across = LANES // wide
    tall = count // pieces_across
    for height, message_ref in enumerate(message_refs):
        chosen = [height] + list(range(inner_bits, heights))
        spans = [slice(height * rank, (height + 1) * rank) for height in chosen]
        powers = [power[:, span] for span in spans]
        powers.append(jnp.zeros((count - len(spans), rank), jnp.float32))
        body = [fixed[:, span] for span in spans] + [jnp.concatenate(powers, axis=0)]
        if wide > rank * len(body):
            body.append(jnp.zeros((count, wide - rank * len(body)), jnp.float32))
        body = jnp.concatenate(body, axis=1)
        body = jnp.concatenate(
            [body[at * tall : (at + 1) * tall] for at in range(pieces_across)], axis=1
        )
        message_ref[4 * sub :] = body.astype(jnp.int32).astype(jnp.int16)


def messages(coords, noise, factors, probes, local_levels, inner_bits):
    levels, _, rank, points = factors.shape
    count = probes.shape[0]
    leaves = points // LEAF
    heights = levels - local_levels
    wide = message_width(rank, heights - inner_bits)
    rows = (4 * points + count * wide) // LANES
    whole = pl.BlockSpec(memory_space=pltpu.VMEM)
    away = pl.BlockSpec(memory_space=pltpu.HBM)
    return pl.pallas_call(
        functools.partial(message_kernel, local_levels, inner_bits),
        in_specs=[away] * 4,
        out_specs=[whole] * inner_bits,
        out_shape=[jax.ShapeDtypeStruct((rows, LANES), jnp.int16)] * inner_bits,
        scratch_shapes=[
            pltpu.VMEM((leaves, heights, rank, LEAF), jnp.bfloat16),
            pltpu.VMEM((leaves, count, LEAF), jnp.bfloat16),
            pltpu.VMEM((3, points), jnp.float32),
            pltpu.VMEM((1, points), jnp.float32),
            pltpu.SemaphoreType.DMA((leaves,)),
            pltpu.SemaphoreType.DMA((leaves,)),
            pltpu.SemaphoreType.DMA((2,)),
        ],
        compiler_params=pltpu.CompilerParams(vmem_limit_bytes=56 * MIB),
        cost_estimate=pl.CostEstimate(
            flops=2 * heights * rank * count * points,
            bytes_accessed=2 * points * (heights * rank + count + 8),
            transcendentals=0,
        ),
    )(factors, probes, coords, noise.reshape(1, points))


def sums_kernel(rank, points, chips, *refs):
    near_refs, far_refs = refs[:chips], refs[chips : 2 * chips]
    lower_ref, outer_refs = refs[2 * chips], refs[2 * chips + 1 :]
    count = lower_ref.shape[0]
    inner_bits = lower_ref.shape[1] // rank
    parts = 1 + len(outer_refs)
    wide = message_width(rank, len(outer_refs))
    lower = [None] * inner_bits
    outer = [None] * len(outer_refs)

    def added(total, value):
        return value if total is None else total + value

    for chip in range(chips):
        for ref in (near_refs[chip], far_refs[chip]):
            body = ref[4 * points // LANES :].astype(jnp.int32).astype(jnp.float32)
            body = jnp.concatenate(
                [body[:, at : at + wide] for at in range(0, LANES, wide)], axis=0
            )
            powers = jnp.exp2(body[:parts, parts * rank : (parts + 1) * rank]) * (1.0 / COEFF_STEPS)
            scales = jnp.concatenate([powers[part : part + 1] for part in range(parts)], axis=1)
            values = body[:, : parts * rank] * scales
            if chip > 0 or ref is far_refs[chip]:
                height = chip.bit_length()
                lower[height] = added(lower[height], values[:, :rank])
            for at in range(len(outer)):
                outer[at] = added(outer[at], values[:, (1 + at) * rank : (2 + at) * rank])
    lower_ref[...] = jnp.concatenate(lower, axis=1).astype(jnp.bfloat16)
    for ref, value in zip(outer_refs, outer):
        ref[...] = value


def group_sums(near, far, rank, points, count, inner_bits, outer_bits):
    whole = pl.BlockSpec(memory_space=pltpu.VMEM)
    lower, *outer = pl.pallas_call(
        functools.partial(sums_kernel, rank, points, len(near)),
        in_specs=[whole] * (2 * len(near)),
        out_specs=[whole] * (1 + outer_bits),
        out_shape=[jax.ShapeDtypeStruct((count, inner_bits * rank), jnp.bfloat16)]
        + [jax.ShapeDtypeStruct((count, rank), jnp.float32)] * outer_bits,
        compiler_params=pltpu.CompilerParams(vmem_limit_bytes=4 * MIB),
    )(*near, *far)
    return lower, outer


def norm_pieces(value):
    high = value.astype(jnp.bfloat16).astype(jnp.float32)
    rest = value - high
    middle = rest.astype(jnp.bfloat16).astype(jnp.float32)
    return [high, middle, rest - middle]


def gather_kernel(chips, me_ref, order_ref, *refs):
    near_refs, far_refs = refs[:chips], refs[chips : 2 * chips]
    across_ref, along_ref, extra_ref, table = refs[2 * chips :]
    points = order_ref.shape[1]
    rows = 4 * points // LANES
    sub = rows // 4
    shards = 2 * chips
    for shard in range(shards):
        source = (near_refs if shard % 2 == 0 else far_refs)[shard // 2]
        whole = source[:rows].astype(jnp.int32) + int(OFFSET)
        high = (whole >> 8).astype(jnp.float32).astype(jnp.bfloat16)
        low = (whole & 255).astype(jnp.float32).astype(jnp.bfloat16)
        table[2 * rows * shard : 2 * rows * shard + rows, :] = high
        table[2 * rows * shard + rows : 2 * rows * (shard + 1), :] = low

    picks = order_ref[...] ^ (me_ref[0] * points)
    lanes = picks & (LANES - 1)
    lines = picks // LANES

    def lookup(start):
        hot = jnp.where(
            lax.broadcasted_iota(jnp.int32, (LANES, TILE), 0) == lanes[:, start : start + TILE],
            1.0,
            0.0,
        ).astype(jnp.bfloat16)
        return jnp.dot(table[...], hot, preferred_element_type=jnp.float32)

    def select(start, looked):
        span = slice(start, start + TILE)
        place = lines[:, span] - lax.broadcasted_iota(jnp.int32, (sub, TILE), 0)
        totals = [jnp.zeros((sub, TILE), jnp.float32) for _ in range(8)]
        for shard in range(shards):
            here = place == shard * sub
            for which in range(8):
                at = 2 * rows * shard + which * sub
                totals[which] = jnp.where(here, looked[at : at + sub], totals[which])
        found = [jnp.sum(total, axis=0, keepdims=True) for total in totals]
        blank = jnp.zeros((5, TILE), jnp.float32)
        high = (jnp.concatenate(found[:3] + [blank], axis=0) - COORD_MIDDLE) * (256.0 * FEATURE_STEP)
        low = jnp.concatenate(found[4:7] + [blank], axis=0) * FEATURE_STEP
        real = lax.broadcasted_iota(jnp.int32, (8, TILE), 0) < 3
        high = jnp.where(real, high, 0.0)
        value = high + low
        norm = norm_pieces(jnp.sum(value * value, axis=0, keepdims=True))
        ones = jnp.ones((3, TILE), jnp.float32)
        pad = jnp.zeros((2, TILE), jnp.float32)
        none = jnp.zeros((8, TILE), jnp.float32)
        across_ref[:, span] = jnp.concatenate(
            [-2.0 * high, -2.0 * low, -2.0 * high, -2.0 * low] + [ones] + norm + [pad, none], axis=0
        ).astype(jnp.bfloat16)
        along = jnp.concatenate([high, high, low, low] + norm + [ones, pad, none], axis=0)
        along_ref[span, :] = along.T.astype(jnp.bfloat16)
        spread = (found[3] * 256.0 + found[7]) * (1.0 / NOISE_SCALE)
        extra_ref[:, span] = (1.0 + spread).astype(jnp.bfloat16).astype(jnp.float32) - 1.0

    starts = list(range(0, points, TILE))
    looked = lookup(starts[0])
    for start in starts[1:]:
        ahead = lookup(start)
        select(start - TILE, looked)
        looked = ahead
    select(starts[-1], looked)


def gathered(me, order, near, far):
    points = order.shape[1]
    chips = len(near)
    whole = pl.BlockSpec(memory_space=pltpu.VMEM)
    return pl.pallas_call(
        functools.partial(gather_kernel, chips),
        in_specs=[pl.BlockSpec(memory_space=pltpu.SMEM)] + [whole] * (1 + 2 * chips),
        out_specs=[whole] * 3,
        out_shape=[
            jax.ShapeDtypeStruct((48, points), jnp.bfloat16),
            jax.ShapeDtypeStruct((points, 48), jnp.bfloat16),
            jax.ShapeDtypeStruct((1, points), jnp.float32),
        ],
        scratch_shapes=[pltpu.VMEM((16 * chips * points // LANES, LANES), jnp.bfloat16)],
        compiler_params=pltpu.CompilerParams(vmem_limit_bytes=16 * MIB),
        cost_estimate=pl.CostEstimate(
            flops=32 * points * chips * points, bytes_accessed=points * 36, transcendentals=0
        ),
    )(me, order, *near, *far)


def dense_kernel(
    across_ref, along_ref, extra_ref, probes_ref, factors_ref, lower_ref, *rest
):
    outer_refs = rest[:-9]
    out_ref, vectors, left, right, blocks, squares, totals, in_sems, out_sems = rest[-9:]
    levels, _, rank, points = factors_ref.shape
    leaves = points // LEAF
    local_levels = right.shape[0]
    arriving = [
        pltpu.make_async_copy(probes_ref, vectors, in_sems.at[0]),
        pltpu.make_async_copy(
            factors_ref.at[pl.ds(0, local_levels), 1], right, in_sems.at[1 + leaves]
        ),
    ]
    for leaf in range(leaves):
        arriving.append(
            pltpu.make_async_copy(
                factors_ref.at[:, 0, :, pl.ds(leaf * LEAF, LEAF)],
                left.at[leaf],
                in_sems.at[1 + leaf],
            )
        )
    for copy in arriving:
        copy.start()

    upper = [lower_ref[...].astype(jnp.float32)]
    for bit in range(len(outer_refs).bit_length()):
        arrived = [ref[...] for ref in outer_refs[(1 << bit) - 1 : (2 << bit) - 1]]
        upper.append(functools.reduce(jnp.add, arrived))
    upper = jnp.concatenate(upper, axis=1)

    def distances(slot, leaf, column):
        base, last = leaf * LEAF, column + TILE
        squares[slot, :last] = jnp.dot(
            along_ref[base : base + last],
            across_ref[:, base + column : base + last],
            preferred_element_type=jnp.float32,
        )

    def entries(slot, leaf, column):
        for row in range(0, column + TILE, STRIP):
            skip = max(row - column, 0)
            square = jnp.maximum(squares[slot, row : row + STRIP, skip:], 1e-30)
            scaled = square * lax.rsqrt(square)
            value = (scaled + 1.0 / LN_2) * jnp.exp2(LOG2_LN_2 - scaled)
            blocks[leaf, row : row + STRIP, column + skip : column + TILE] = value.astype(
                jnp.bfloat16
            )
            if row == column:
                mirrored = value[:, STRIP:].T.astype(jnp.bfloat16)
                blocks[leaf, row + STRIP : row + TILE, column : column + STRIP] = mirrored

    def products(leaf, column):
        base, last = leaf * LEAF, column + TILE
        here = vectors[:, base + column : base + last]
        total = here.astype(jnp.float32) * extra_ref[:, base + column : base + last]
        totals[leaf, :, column:last] = total + jnp.dot(
            vectors[:, base : base + last],
            blocks[leaf, :last, column:last],
            preferred_element_type=jnp.float32,
        )
        if column > 0:
            totals[leaf, :, :column] += lax.dot_general(
                here,
                blocks[leaf, :column, column:last],
                (((1,), (1,)), ((), ())),
                preferred_element_type=jnp.float32,
            )

    def own_coefficients(leaf):
        span = slice(leaf * LEAF, (leaf + 1) * LEAF)
        return lax.dot_general(
            right[:, :, span].reshape(local_levels * rank, LEAF),
            vectors[:, span],
            (((1,), (1,)), ((), ())),
            preferred_element_type=jnp.float32,
        )

    def local_siblings(leaf, coeffs):
        parts = []
        for level in range(local_levels):
            node = (leaf >> level) ^ 1
            members = coeffs[node << level : (node + 1) << level]
            parts.append(functools.reduce(jnp.add, members)[level * rank : (level + 1) * rank])
        return jnp.concatenate(parts, axis=0).T

    def low_rank(leaf):
        both = jnp.concatenate([local_siblings(leaf, coeffs), upper], axis=1)
        totals[leaf] += jnp.dot(
            both.astype(jnp.bfloat16),
            left[leaf].reshape(levels * rank, LEAF),
            preferred_element_type=jnp.float32,
        )

    leaving = []
    coeffs = []
    ready = None
    order = [(leaf, column) for leaf in range(leaves) for column in range(0, LEAF, TILE)]
    distances(0, *order[0])
    for at, (leaf, column) in enumerate(order):
        if at + 1 < len(order):
            distances((at + 1) % 2, *order[at + 1])
        entries(at % 2, leaf, column)
        if ready is not None:
            if ready == (0, 0):
                for copy in arriving:
                    copy.wait()
                coeffs = [own_coefficients(each) for each in range(leaves)]
            products(*ready)
            if ready[1] + TILE == LEAF:
                low_rank(ready[0])
                leaving.append(sent_out(totals, out_ref, out_sems, ready[0]))
        ready = (leaf, column)
    products(*ready)
    low_rank(ready[0])
    leaving.append(sent_out(totals, out_ref, out_sems, ready[0]))
    for copy in leaving:
        copy.wait()


def sent_out(totals, out_ref, sems, leaf):
    copy = pltpu.make_async_copy(
        totals.at[leaf], out_ref.at[:, pl.ds(leaf * LEAF, LEAF)], sems.at[leaf]
    )
    copy.start()
    return copy


def assembled(features, probes, factors, lower, outer, local_levels):
    count, points = probes.shape
    levels, _, rank, _ = factors.shape
    leaves = points // LEAF
    whole = pl.BlockSpec(memory_space=pltpu.VMEM)
    away = pl.BlockSpec(memory_space=pltpu.HBM)
    return pl.pallas_call(
        dense_kernel,
        in_specs=[whole, whole, whole, away, away, whole] + [whole] * len(outer),
        out_specs=away,
        out_shape=jax.ShapeDtypeStruct((count, points), jnp.float32),
        scratch_shapes=[
            pltpu.VMEM((count, points), jnp.bfloat16),
            pltpu.VMEM((leaves, levels, rank, LEAF), jnp.bfloat16),
            pltpu.VMEM((local_levels, rank, points), jnp.bfloat16),
            pltpu.VMEM((leaves, LEAF, LEAF), jnp.bfloat16),
            pltpu.VMEM((2, LEAF, TILE), jnp.float32),
            pltpu.VMEM((leaves, count, LEAF), jnp.float32),
            pltpu.SemaphoreType.DMA((2 + leaves,)),
            pltpu.SemaphoreType.DMA((leaves,)),
        ],
        compiler_params=pltpu.CompilerParams(vmem_limit_bytes=32 * MIB),
        cost_estimate=pl.CostEstimate(
            flops=2 * points * (LEAF * count + levels * rank * count),
            bytes_accessed=points * (2 * levels * rank + 6 * count),
            transcendentals=points * LEAF,
        ),
    )(*features, probes, factors, lower, *outer)


def local(coords, noise, order, probes, factors):
    count, points = probes.shape
    rank = factors.shape[2]
    local_levels = (points // LEAF).bit_length() - 1
    inner_bits = lax.axis_size("gy").bit_length() - 1
    outer_bits = lax.axis_size("gx").bit_length() - 1
    sent = messages(coords, noise, factors, probes, local_levels, inner_bits)
    me = lax.axis_index("gy")
    chips = 1 << (inner_bits - 1)
    arrived = {
        chip: exchanged(sent[chip.bit_length()], "gy", 2 * chip) for chip in range(chips - 1, 0, -1)
    }
    own = sent[0] ^ (me >> 8).astype(jnp.int16)
    others = [arrived[chip] for chip in range(1, chips)]
    near = [own] + others
    far = [exchanged(part, "gy", 1) for part in [sent[0]] + others]
    lower, partial = group_sums(near, far, rank, points, count, inner_bits, outer_bits)
    outer = [
        exchanged(partial[mask.bit_length() - 1], "gx", mask) for mask in range(1, 1 << outer_bits)
    ]
    features = gathered(me.reshape(1), order, near, far)
    return assembled(features, probes, factors, lower, outer, local_levels)


def solution(mesh):
    return jax.shard_map(
        local,
        mesh=mesh,
        in_specs=(
            P(None, ("gx", "gy")),
            P(("gx", "gy")),
            P("gx", "gy"),
            P(None, ("gx", "gy")),
            P(None, None, None, ("gx", "gy")),
        ),
        out_specs=P(None, ("gx", "gy")),
        check_vma=False,
    )
```

time: 254 us -> 28.8 us (0.11)
  blocking collectives: 156 us -> 0 us
  local copies, waits for them, and re-layouts: 45.2 us -> 0.01 us
  matrix products: 28.9 us -> 0 us
  Pallas kernels: 0 us -> 11.7 us
  starting transfers between devices: 17.7 us -> 9.75 us
    all_gather x2 -> x0, blocking collectives: 156 us -> none  [the longest x1 140 us: local(): lax.all_gather(coords, 'gy', axis=1, tiled=True)]
    gather x2 -> x0, local copies, waits for them, and re-layouts: 39.6 us -> none  [the longest x1 23 us: local(): tree_noise = jnp.take(whole_noise, picks, axis=0)]
    dot_general x18 -> x0, matrix products: 28.9 us -> none  [the longest x4 13.3 us: local(): jnp.dot(probes[:, start:start + LEAF], kernel, preferred_element_type=jnp...]
    pallas_call x0 -> x4, Pallas kernels: none -> 11.7 us  [the longest x1 5.74 us: assembled(): pl.pallas_call(dense_kernel, in_specs=[whole, whole, whole, away, away, w...]
    ppermute x15 -> x10, starting transfers between devices: 17.7 us -> 9.75 us  [exchanged(): lax.ppermute(array, axis, [(i, i ^ mask) for i in range(lax.axis_size(axi...]
    slice x3 -> x0, local copies, waits for them, and re-layouts: 4.06 us -> none  [the longest x1 2.8 us: leaf_kernel(): square = (spots[0][:, None] - spots[0][None, :]) ** 2]
    ppermute x15 -> x10, waiting for transfers between devices: 3.7 us -> 6.22 us  [exchanged(): lax.ppermute(array, axis, [(i, i ^ mask) for i in range(lax.axis_size(axi...]
  transfers between devices with their start and end apart: 15 -> 10, of which waited for: 6 -> 4; matrix products, arithmetic and copies ran while one was open for 29% -> 3% of each run, Pallas kernels for 0% -> 9%
where the time goes in v1:
time: 28.8 us; the launch traced here: 28.6 us
  Pallas kernels  11.7 us (41%)
  starting transfers between devices  9.75 us (34%)
  waiting for transfers between devices  6.22 us (22%)
  other arithmetic  0.81 us (3%)
    ppermute x10, starting transfers between devices, exchanged(): lax.ppermute(array, axis, [(i, i ^ mask) for i in range(lax.axis_size(axi...  9.75 us
    ppermute x10, waiting for transfers between devices, exchanged(): lax.ppermute(array, axis, [(i, i ^ mask) for i in range(lax.axis_size(axi...  6.22 us
    pallas_call x1, Pallas kernels, assembled(): pl.pallas_call(dense_kernel, in_specs=[whole, whole, whole, away, away, w...  5.74 us
    pallas_call x1, Pallas kernels, messages(): pl.pallas_call(functools.partial(message_kernel, local_levels, inner_bits...  3.16 us
    pallas_call x1, Pallas kernels, gathered(): pl.pallas_call(functools.partial(gather_kernel, chips), in_specs=[pl.Bloc...  2.64 us
    xor x1, other arithmetic, local(): own = sent[0] ^ (me >> 8).astype(jnp.int16)  0.81 us
  transfers between devices with their start and end apart: 10, of which 4 were waited for; matrix products, arithmetic and copies ran while one was open for 3% of the time, Pallas kernels for 9%

profile of v1, /device:TPU:0, one launch (start us, length us, event | category | flops | bytes accessed | tf_op | source)
XLA Modules:
  0.0 28.6 jit_solution(14245485623311564772)
XLA Ops:
  0.0 0.0 copy-start.2
  0.0 3.2 %shard_map.55 = (s16[96,256]{1,0:T(8,128)(2,1)}, s16[96,256]{1,0:T(8,128)(2,1)}, s16[96,256]{1,0:T(8,128)(2,1)}) custom-call(bf16[7,2,32,4096]{3,2,1,0:T(8,128)(2,1)} %factors_ref.3, bf16[64,4096]{1,0:T(8,128)(2,1)} %probes_ref.3, f32[3,4096]{1,0:T(4,128)} %coords_ref.1, f32[1,4096]{1,0:T(1,128)} %bitcast.2), custom_call_target="tpu_custom_call" | custom-call | flops 83886080 | bytes 1900544 | tf_op jit(solution)/shard_map/pallas_call | solution.py:131
  3.2 3.1 %collective-permute-start = (s16[96,256]{1,0:T(8,128)(2,1)}, s16[96,256]{1,0:T(8,128)(2,1)S(1)}, u32[]{:S(2)}, u32[]{:S(2)}) collective-permute-start(s16[96,256]{1,0:T(8,128)(2,1)} %get-tuple-element.15), channel_id=1, source_target_pairs={{0,2},{1,3},{2,0},{3,1},{4,6},{5,7},{6,4},{7,5},{8,10},{9,11},{10,... | collective-permute-start | bytes 147464 | tf_op jit(solution)/shard_map/ppermute | solution.py:28
  6.3 2.5 %collective-permute-start.2 = (s16[96,256]{1,0:T(8,128)(2,1)}, s16[96,256]{1,0:T(8,128)(2,1)S(1)}, u32[]{:S(2)}, u32[]{:S(2)}) collective-permute-start(s16[96,256]{1,0:T(8,128)(2,1)} %get-tuple-element.16), channel_id=1, source_target_pairs={{0,6},{1,7},{2,4},{3,5},{4,2},{5,3},{6,0},{7,1},{8,14},{9,15},{10,... | collective-permute-start | bytes 147464 | tf_op jit(solution)/shard_map/ppermute | solution.py:28
  8.7 0.1 collective-permute-start.1
  8.9 0.0 collective-permute-start.3
  8.9 0.0 collective-permute-done.refs_1_
  8.9 0.5 %collective-permute-start.4 = (s16[96,256]{1,0:T(8,128)(2,1)S(1)}, s16[96,256]{1,0:T(8,128)(2,1)S(1)}, u32[]{:S(2)}, u32[]{:S(2)}) collective-permute-start(s16[96,256]{1,0:T(8,128)(2,1)S(1)} %collective-permute-done.refs_1_), channel_id=1, source_target_pairs={{0,1},{1,0},{2,3},{3,2},{4,5},{5,4},{6,7},{7,6},{8,9},{9,8},{10,11... | collective-permute-start | bytes 147464 | tf_op jit(solution)/shard_map/ppermute | solution.py:28
  9.4 3.6 %collective-permute-done.2.refs_3_ = s16[96,256]{1,0:T(8,128)(2,1)S(1)} collective-permute-done((s16[96,256]{1,0:T(8,128)(2,1)}, s16[96,256]{1,0:T(8,128)(2,1)S(1)}, u32[]{:S(2)}, u32[]{:S(2)}) %collective-permute-start.2) | collective-permute-done | bytes 49184 | tf_op jit(solution)/shard_map/ppermute | solution.py:28
  13.0 0.0 collective-permute-start.6
  13.0 1.5 %collective-permute-done.1.refs_2_ = s16[96,256]{1,0:T(8,128)(2,1)S(1)} collective-permute-done((s16[96,256]{1,0:T(8,128)(2,1)}, s16[96,256]{1,0:T(8,128)(2,1)S(1)}, u32[]{:S(2)}, u32[]{:S(2)}) %collective-permute-start.1) | collective-permute-done | bytes 49184 | tf_op jit(solution)/shard_map/ppermute | solution.py:28
  14.5 0.0 collective-permute-start.5
  14.5 0.8 %broadcast_xor_fusion.refs_0_ = s16[96,256]{1,0:T(8,128)(2,1)S(1)} fusion(s16[96,256]{1,0:T(8,128)(2,1)} %get-tuple-element.14, s16[]{:T(256)S(6)} %convert_element_type.3), kind=kLoop, calls=%fused_computation | loop fusion | flops 24576 | bytes 98306 | tf_op jit(solution)/shard_map/xor | solution.py:461
  15.3 0.0 collective-permute-done.3.refs_4_
  15.3 0.0 collective-permute-done.4.refs_5_
  15.3 0.0 collective-permute-done.6.refs_7_
  15.3 0.4 %collective-permute-done.5.refs_6_ = s16[96,256]{1,0:T(8,128)(2,1)S(1)} collective-permute-done((s16[96,256]{1,0:T(8,128)(2,1)S(1)}, s16[96,256]{1,0:T(8,128)(2,1)S(1)}, u32[]{:S(2)}, u32[]{:S(2)}) %collective-permute-start.5) | collective-permute-done | bytes 49184 | tf_op jit(solution)/shard_map/ppermute | solution.py:28
  15.7 0.2 shard_map.57
  15.9 2.5 %collective-permute-start.9 = (f32[64,32]{1,0:T(8,128)S(1)}, f32[64,32]{1,0:T(8,128)S(1)}, u32[]{:S(2)}, u32[]{:S(2)}) collective-permute-start(f32[64,32]{1,0:T(8,128)S(1)} %get-tuple-element.22), channel_id=1, source_target_pairs={{0,24},{8,16},{16,8},{24,0},{1,25},{9,17},{17,9},{25,1},{2,26},{10... | collective-permute-start | bytes 24584 | tf_op jit(solution)/shard_map/ppermute | solution.py:28
  18.4 0.5 %collective-permute-start.8 = (f32[64,32]{1,0:T(8,128)S(1)}, f32[64,32]{1,0:T(8,128)S(1)}, u32[]{:S(2)}, u32[]{:S(2)}) collective-permute-start(f32[64,32]{1,0:T(8,128)S(1)} %get-tuple-element.22), channel_id=1, source_target_pairs={{0,16},{8,24},{16,0},{24,8},{1,17},{9,25},{17,1},{25,9},{2,18},{10... | collective-permute-start | bytes 24584 | tf_op jit(solution)/shard_map/ppermute | solution.py:28
  18.9 0.5 %collective-permute-start.7 = (f32[64,32]{1,0:T(8,128)S(1)}, f32[64,32]{1,0:T(8,128)S(1)}, u32[]{:S(2)}, u32[]{:S(2)}) collective-permute-start(f32[64,32]{1,0:T(8,128)S(1)} %get-tuple-element.21), channel_id=1, source_target_pairs={{0,8},{8,0},{16,24},{24,16},{1,9},{9,1},{17,25},{25,17},{2,10},{10... | collective-permute-start | bytes 24584 | tf_op jit(solution)/shard_map/ppermute | solution.py:28
  19.4 0.0 copy-done.2
  19.4 0.0 copy-start
  19.4 0.0 copy-start.1
  19.5 2.6 %shard_map.56 = (bf16[48,4096]{1,0:T(8,128)(2,1)S(1)}, bf16[4096,48]{1,0:T(8,128)(2,1)S(1)}, f32[1,4096]{1,0:T(1,128)S(1)}) custom-call(s32[1]{0:T(128)} %bitcast.me_ref, s32[1,4096]{1,0:T(1,128)S(1)} %copy-done.2, s16[96,256]{1,0:T(8,128)(2,1)S(1)} %broadcast_xor_fusion.refs_0_, s16[96,256]{1,0:T(8,128)(2,1)S(1)} %collective-permute-done.refs_1_, ...), custom_call_target="tpu_custom_call" | custom-call | flops 2147483648 | bytes 147456 | tf_op jit(solution)/shard_map/pallas_call | solution.py:274
  22.1 0.7 %collective-permute-done.7.rest_0_ = f32[64,32]{1,0:T(8,128)S(1)} collective-permute-done((f32[64,32]{1,0:T(8,128)S(1)}, f32[64,32]{1,0:T(8,128)S(1)}, u32[]{:S(2)}, u32[]{:S(2)}) %collective-permute-start.7) | collective-permute-done | bytes 8224 | tf_op jit(solution)/shard_map/ppermute | solution.py:28
  22.8 0.0 collective-permute-done.9.rest_2_
  22.8 0.0 collective-permute-done.8.rest_1_
  22.8 0.0 copy-done
  22.8 0.0 copy-done.1
  22.8 5.7 %shard_map.58 = f32[64,4096]{1,0:T(8,128)} custom-call(bf16[48,4096]{1,0:T(8,128)(2,1)S(1)} %get-tuple-element.17.across_ref, bf16[4096,48]{1,0:T(8,128)(2,1)S(1)} %get-tuple-element.18.along_ref, f32[1,4096]{1,0:T(1,128)S(1)} %get-tuple-element.19.extra_ref, bf16[64,4096]{1,0:T(8,128)(2,1)S(1)} %copy-done.1, bf16[7,2,32,4096]{3,2,1,0:T(8,128)(2,1)S(1)} %copy-done, ...), custom_call_target="tpu_custom_call" | custom-call | flops 654311424 | bytes 3407872 | tf_op jit(solution)/shard_map/pallas_call | solution.py:425
Async XLA Ops:
  0.0 19.4 %copy-start.2 = (s32[1,4096]{1,0:T(1,128)S(1)}, s32[1,4096]{1,0:T(1,128)}, u32[]{:S(2)}) copy-start(s32[1,4096]{1,0:T(1,128)} %order_ref.1) | copy-start | bytes 49156
  3.2 5.7 %collective-permute-start = (s16[96,256]{1,0:T(8,128)(2,1)}, s16[96,256]{1,0:T(8,128)(2,1)S(1)}, u32[]{:S(2)}, u32[]{:S(2)}) collective-permute-start(s16[96,256]{1,0:T(8,128)(2,1)} %get-tuple-element.15), channel_id=1, source_target_pairs={{0,2},{1,3},{2,0},{3,1},{4,6},{5,7},{6,4},{7,5},{8,10},{9,11},{10,... | collective-permute-start | bytes 147464 | tf_op jit(solution)/shard_map/ppermute | solution.py:28
  6.3 6.7 %collective-permute-start.2 = (s16[96,256]{1,0:T(8,128)(2,1)}, s16[96,256]{1,0:T(8,128)(2,1)S(1)}, u32[]{:S(2)}, u32[]{:S(2)}) collective-permute-start(s16[96,256]{1,0:T(8,128)(2,1)} %get-tuple-element.16), channel_id=1, source_target_pairs={{0,6},{1,7},{2,4},{3,5},{4,2},{5,3},{6,0},{7,1},{8,14},{9,15},{10,... | collective-permute-start | bytes 147464 | tf_op jit(solution)/shard_map/ppermute | solution.py:28
  8.7 5.7 %collective-permute-start.1 = (s16[96,256]{1,0:T(8,128)(2,1)}, s16[96,256]{1,0:T(8,128)(2,1)S(1)}, u32[]{:S(2)}, u32[]{:S(2)}) collective-permute-start(s16[96,256]{1,0:T(8,128)(2,1)} %get-tuple-element.16), channel_id=1, source_target_pairs={{0,4},{1,5},{2,6},{3,7},{4,0},{5,1},{6,2},{7,3},{8,12},{9,13},{10,... | collective-permute-start | bytes 147464 | tf_op jit(solution)/shard_map/ppermute | solution.py:28
  8.9 6.4 %collective-permute-start.3 = (s16[96,256]{1,0:T(8,128)(2,1)}, s16[96,256]{1,0:T(8,128)(2,1)S(1)}, u32[]{:S(2)}, u32[]{:S(2)}) collective-permute-start(s16[96,256]{1,0:T(8,128)(2,1)} %get-tuple-element.14), channel_id=1, source_target_pairs={{0,1},{1,0},{2,3},{3,2},{4,5},{5,4},{6,7},{7,6},{8,9},{9,8},{10,11... | collective-permute-start | bytes 147464 | tf_op jit(solution)/shard_map/ppermute | solution.py:28
  8.9 6.4 %collective-permute-start.4 = (s16[96,256]{1,0:T(8,128)(2,1)S(1)}, s16[96,256]{1,0:T(8,128)(2,1)S(1)}, u32[]{:S(2)}, u32[]{:S(2)}) collective-permute-start(s16[96,256]{1,0:T(8,128)(2,1)S(1)} %collective-permute-done.refs_1_), channel_id=1, source_target_pairs={{0,1},{1,0},{2,3},{3,2},{4,5},{5,4},{6,7},{7,6},{8,9},{9,8},{10,11... | collective-permute-start | bytes 147464 | tf_op jit(solution)/shard_map/ppermute | solution.py:28
  13.0 2.3 %collective-permute-start.6 = (s16[96,256]{1,0:T(8,128)(2,1)S(1)}, s16[96,256]{1,0:T(8,128)(2,1)S(1)}, u32[]{:S(2)}, u32[]{:S(2)}) collective-permute-start(s16[96,256]{1,0:T(8,128)(2,1)S(1)} %collective-permute-done.2.refs_3_), channel_id=1, source_target_pairs={{0,1},{1,0},{2,3},{3,2},{4,5},{5,4},{6,7},{7,6},{8,9},{9,8},{10,11... | collective-permute-start | bytes 147464 | tf_op jit(solution)/shard_map/ppermute | solution.py:28
  14.5 1.2 %collective-permute-start.5 = (s16[96,256]{1,0:T(8,128)(2,1)S(1)}, s16[96,256]{1,0:T(8,128)(2,1)S(1)}, u32[]{:S(2)}, u32[]{:S(2)}) collective-permute-start(s16[96,256]{1,0:T(8,128)(2,1)S(1)} %collective-permute-done.1.refs_2_), channel_id=1, source_target_pairs={{0,1},{1,0},{2,3},{3,2},{4,5},{5,4},{6,7},{7,6},{8,9},{9,8},{10,11... | collective-permute-start | bytes 147464 | tf_op jit(solution)/shard_map/ppermute | solution.py:28
  15.9 6.9 %collective-permute-start.9 = (f32[64,32]{1,0:T(8,128)S(1)}, f32[64,32]{1,0:T(8,128)S(1)}, u32[]{:S(2)}, u32[]{:S(2)}) collective-permute-start(f32[64,32]{1,0:T(8,128)S(1)} %get-tuple-element.22), channel_id=1, source_target_pairs={{0,24},{8,16},{16,8},{24,0},{1,25},{9,17},{17,9},{25,1},{2,26},{10... | collective-permute-start | bytes 24584 | tf_op jit(solution)/shard_map/ppermute | solution.py:28
  18.4 4.4 %collective-permute-start.8 = (f32[64,32]{1,0:T(8,128)S(1)}, f32[64,32]{1,0:T(8,128)S(1)}, u32[]{:S(2)}, u32[]{:S(2)}) collective-permute-start(f32[64,32]{1,0:T(8,128)S(1)} %get-tuple-element.22), channel_id=1, source_target_pairs={{0,16},{8,24},{16,0},{24,8},{1,17},{9,25},{17,1},{25,9},{2,18},{10... | collective-permute-start | bytes 24584 | tf_op jit(solution)/shard_map/ppermute | solution.py:28
  18.9 3.9 %collective-permute-start.7 = (f32[64,32]{1,0:T(8,128)S(1)}, f32[64,32]{1,0:T(8,128)S(1)}, u32[]{:S(2)}, u32[]{:S(2)}) collective-permute-start(f32[64,32]{1,0:T(8,128)S(1)} %get-tuple-element.21), channel_id=1, source_target_pairs={{0,8},{8,0},{16,24},{24,16},{1,9},{9,1},{17,25},{25,17},{2,10},{10... | collective-permute-start | bytes 24584 | tf_op jit(solution)/shard_map/ppermute | solution.py:28
  19.4 3.4 %copy-start = (bf16[7,2,32,4096]{3,2,1,0:T(8,128)(2,1)S(1)}, bf16[7,2,32,4096]{3,2,1,0:T(8,128)(2,1)}, u32[]{:S(2)}) copy-start(bf16[7,2,32,4096]{3,2,1,0:T(8,128)(2,1)} %factors_ref.3) | copy-start | bytes 11010052
  19.4 3.4 %copy-start.1 = (bf16[64,4096]{1,0:T(8,128)(2,1)S(1)}, bf16[64,4096]{1,0:T(8,128)(2,1)}, u32[]{:S(2)}) copy-start(bf16[64,4096]{1,0:T(8,128)(2,1)} %probes_ref.3) | copy-start | bytes 1572868
